TPU v7x, 256 devices: a whole 4x4x8 slice. The times are simulated.
256 devices in a mesh: face: 128 (over x, y_hi, z, core), sub: 2 (over y_lo).
Axes of the slice: x: 4, y: 4 (y_hi: 2, y_lo: 2; y = y_hi * 2 + y_lo), z: 8, core: 2. Of those that a mesh axis runs over, the one named last changes fastest.
Arguments:
- inputs: bfloat16 [128, 2, 64, 64, 128], P('face', 'sub'), may hold values from -6 to 6
- kernel_one: bfloat16 [3, 3, 128, 128], replicated, may hold values from -0.1875 to 0.1875
- kernel_two: bfloat16 [3, 3, 128, 128], replicated, may hold values from -0.1875 to 0.1875
- cotangent: bfloat16 [128, 2, 64, 64, 128], P('face', 'sub'), may hold values from -6 to 6
- edge_codes: int32 [128, 2, 4], replicated, may hold values from 0 to 7
- corner_codes: int32 [128, 2, 4], replicated, may hold values from 0 to 3
Outputs:
- outputs: bfloat16 [128, 2, 64, 64, 128], P('face', 'sub')
- grad_inputs: bfloat16 [128, 2, 64, 64, 128], P('face', 'sub')
- grad_kernel_one: float32 [3, 3, 128, 128], replicated
- grad_kernel_two: float32 [3, 3, 128, 128], replicated
All inputs are finite; a program needn't handle non-finite values.
Results may differ from a plain program's by a relative error of at most 0.005.
Values may be sent and summed in bfloat16 or wider, within the bound.
No kernel may reach another device: no remote copies, remote signals or barrier semaphores. Data moves between devices by JAX's collectives and lax.ppermute only.
A program may use at most 128 MiB of HBM per device.

v0:
```python
import math
import jax
import jax.numpy as jnp
from jax import lax
from jax.sharding import PartitionSpec as P

GRID_ROWS = 8


def shifted(x, axis, by):
    size = lax.axis_size(axis)
    return lax.ppermute(x, axis, [(i, (i + by) % size) for i in range(size)])


def neighbour_steps():
    row_width = lax.axis_size("face") // GRID_ROWS * lax.axis_size("sub")
    return (
        [-row_width, 1, row_width, -1],
        [-row_width - 1, -row_width + 1, row_width + 1, row_width - 1],
    )


def pull_sets(payload, offset):
    return shifted(payload, ("face", "sub"), offset)


def back_sets(payload, offset):
    return shifted(payload, ("face", "sub"), offset)


def fill_halo(fields, edge_codes, corner_codes):
    device_count = lax.axis_size(("face", "sub"))
    own_index = lax.axis_index(("face", "sub"))
    side_len = fields.shape[1]
    edge_table = edge_codes.reshape(device_count, 4)
    corner_table = corner_codes.reshape(device_count, 4)
    edge_steps, corner_steps = neighbour_steps()
    edge_sets = jnp.stack([fields[0, 0], fields[0, :, -1], fields[0, -1], fields[0, :, 0]])
    corner_sets = jnp.stack(
        [fields[0, 0, 0], fields[0, 0, -1], fields[0, -1, -1], fields[0, -1, 0]]
    )
    strips = []
    corner_vals = []
    for direction in range(4):
        arrived = pull_sets(edge_sets, -edge_steps[direction])
        edge_code = edge_table[own_index, direction]
        picked = lax.dynamic_index_in_dim(arrived, edge_code % 4, 0, keepdims=False)
        strips.append(jnp.where(edge_code >= 4, picked[::-1], picked))
    for corner in range(4):
        arrived = pull_sets(corner_sets, -corner_steps[corner])
        corner_vals.append(
            lax.dynamic_index_in_dim(arrived, corner_table[own_index, corner], 0, keepdims=False)
        )
    padded = jnp.pad(fields, ((0, 0), (1, 1), (1, 1), (0, 0)))
    last = side_len + 1
    padded = padded.at[0, 0, 1:last].set(strips[0]).at[0, 1:last, last].set(strips[1])
    padded = padded.at[0, last, 1:last].set(strips[2]).at[0, 1:last, 0].set(strips[3])
    padded = padded.at[0, 0, 0].set(corner_vals[0]).at[0, 0, last].set(corner_vals[1])
    padded = padded.at[0, last, last].set(corner_vals[2]).at[0, last, 0].set(corner_vals[3])
    return padded


def return_halo(grad_pad, edge_codes, corner_codes):
    device_count = lax.axis_size(("face", "sub"))
    own_index = lax.axis_index(("face", "sub"))
    edge_table = edge_codes.reshape(device_count, 4)
    corner_table = corner_codes.reshape(device_count, 4)
    edge_steps, corner_steps = neighbour_steps()
    interior = grad_pad[:, 1:-1, 1:-1]
    pad_strips = [
        grad_pad[0, 0, 1:-1],
        grad_pad[0, 1:-1, -1],
        grad_pad[0, -1, 1:-1],
        grad_pad[0, 1:-1, 0],
    ]
    pad_cells = [grad_pad[0, 0, 0], grad_pad[0, 0, -1], grad_pad[0, -1, -1], grad_pad[0, -1, 0]]
    slot_ids = jnp.arange(4, dtype=jnp.int32)
    edge_add = jnp.zeros((4,) + pad_strips[0].shape, jnp.float32)
    corner_add = jnp.zeros((4,) + pad_cells[0].shape, jnp.float32)
    for direction in range(4):
        edge_code = edge_table[own_index, direction]
        returned = jnp.where(edge_code >= 4, pad_strips[direction][::-1], pad_strips[direction])
        slots = (slot_ids == edge_code % 4).astype(jnp.float32)
        edge_add = edge_add + back_sets(
            slots[:, None, None] * returned[None], edge_steps[direction]
        )
    for corner in range(4):
        slots = (slot_ids == corner_table[own_index, corner]).astype(jnp.float32)
        corner_add = corner_add + back_sets(
            slots[:, None] * pad_cells[corner][None], corner_steps[corner]
        )
    interior = interior.at[0, 0, :].add(edge_add[0]).at[0, :, -1].add(edge_add[1])
    interior = interior.at[0, -1, :].add(edge_add[2]).at[0, :, 0].add(edge_add[3])
    interior = interior.at[0, 0, 0].add(corner_add[0]).at[0, 0, -1].add(corner_add[1])
    interior = interior.at[0, -1, -1].add(corner_add[2]).at[0, -1, 0].add(corner_add[3])
    return interior


def conv_forward(padded, kernel):
    return lax.conv_general_dilated(
        padded,
        kernel,
        (1, 1),
        "VALID",
        dimension_numbers=("NHWC", "HWIO", "NHWC"),
        preferred_element_type=jnp.float32,
    )


def conv_inputs(upstream, kernel):
    widened = jnp.pad(upstream, ((0, 0), (2, 2), (2, 2), (0, 0)))
    turned = jnp.transpose(jnp.flip(kernel, (0, 1)), (0, 1, 3, 2))
    return lax.conv_general_dilated(
        widened,
        turned,
        (1, 1),
        "VALID",
        dimension_numbers=("NHWC", "HWIO", "NHWC"),
        preferred_element_type=jnp.float32,
    )


def conv_kernel(padded, upstream):
    side_len = upstream.shape[1]
    chans = upstream.shape[-1]
    flat_up = upstream.reshape(-1, chans)
    rows_out = []
    for row_off in range(3):
        cols_out = []
        for col_off in range(3):
            window = padded[
                :, row_off : row_off + side_len, col_off : col_off + side_len, :
            ].reshape(-1, chans)
            cols_out.append(
                lax.dot_general(
                    window, flat_up, (((0,), (0,)), ((), ())), preferred_element_type=jnp.float32
                )
            )
        rows_out.append(jnp.stack(cols_out))
    return jnp.stack(rows_out)


def local(inputs, kernel_one, kernel_two, cotangent, edge_codes, corner_codes):
    fields = inputs[0]
    upstream = cotangent[0]
    side_len = fields.shape[1]
    norm_factor = 1.0 / math.sqrt(lax.axis_size(("face", "sub")) * side_len * side_len)
    padded_one = fill_halo(fields, edge_codes, corner_codes)
    preact = conv_forward(padded_one, kernel_one)
    hidden = jax.nn.silu(preact).astype(jnp.bfloat16)
    padded_two = fill_halo(hidden, edge_codes, corner_codes)
    outputs = conv_forward(padded_two, kernel_two).astype(jnp.bfloat16)
    grad_two = conv_kernel(padded_two, upstream)
    grad_hidden = return_halo(conv_inputs(upstream, kernel_two), edge_codes, corner_codes)
    sigmoid_vals = jax.nn.sigmoid(preact)
    grad_pre = (grad_hidden * sigmoid_vals * (1.0 + preact * (1.0 - sigmoid_vals))).astype(
        jnp.bfloat16
    )
    grad_one = conv_kernel(padded_one, grad_pre)
    grad_fields = return_halo(conv_inputs(grad_pre, kernel_one), edge_codes, corner_codes).astype(
        jnp.bfloat16
    )
    grad_one, grad_two = lax.psum((grad_one, grad_two), ("face", "sub"))
    return (outputs[None], grad_fields[None], grad_one * norm_factor, grad_two * norm_factor)


def solution(mesh):
    in_specs = (
        P("face", "sub", None, None, None),
        P(),
        P(),
        P("face", "sub", None, None, None),
        P(),
        P(),
    )
    out_specs = (P("face", "sub", None, None, None), P("face", "sub", None, None, None), P(), P())
    return jax.shard_map(local, mesh=mesh, in_specs=in_specs, out_specs=out_specs, check_vma=False)
```

profile of v0, /device:TPU:8, one launch (start us, length us, event | category | flops | bytes accessed | tf_op | source)
XLA Modules:
  0.0 517.0 jit_solution(1585408178761811315)
XLA Ops:
  8.0 3.3 collective-permute-start.7
  12.3 5.7 %collective-permute-start.5 = (bf16[4,128]{1,0:T(4,128)(2,1)S(1)}, bf16[4,128]{1,0:T(4,128)(2,1)S(1)}, u32[]{:S(2)}, u32[]{:S(2)}) collective-permute-start(bf16[4,128]{1,0:T(4,128)(2,1)S(1)} %pad_maximum_fusion.4), channel_id=1, source_target_pairs={{0,31},{1,32},{2,33},{3,34},{4,35},{5,36},{6,37},{7,38},{8,39},{9,... | collective-permute-start | bytes 3080 | tf_op jit(solution)/shard_map/ppermute | solution.py:12
  33.0 1.9 copy.179
  35.9 3.1 convolution_select_fusion.1
  44.6 2.0 and_reduce_fusion
  51.7 1.7 slice.1266
  53.4 1.5 pad.122
  57.4 4.2 collective-permute-start.20
  61.8 4.5 collective-permute-start.23
  66.4 3.7 collective-permute-start.2
  70.1 4.6 collective-permute-start.1
  75.1 4.6 collective-permute-start.19
  80.3 2.3 collective-permute-done
  82.7 5.7 %collective-permute-start.16 = (f32[4,64,128]{2,1,0:T(8,128)S(1)}, f32[4,64,128]{2,1,0:T(8,128)S(1)}, u32[]{:S(2)}, u32[]{:S(2)}) collective-permute-start(f32[4,64,128]{2,1,0:T(8,128)S(1)} %broadcast_multiply_fusion.9), channel_id=1, source_target_pairs={{0,224},{1,225},{2,226},{3,227},{4,228},{5,229},{6,230},{7,231},{8... | collective-permute-start | bytes 393224 | tf_op jit(solution)/shard_map/ppermute | solution.py:12
  90.0 1.4 scatter.54
  91.3 1.7 scatter.55
  93.0 1.4 scatter.56
  94.4 1.7 scatter.59
  97.3 1.3 scatter.61
  99.7 1.3 scatter.65
  101.0 1.4 copy.155
  103.2 5.0 add_divide_fusion
  111.0 1.8 copy.116
  113.3 1.9 copy.117
  115.2 2.2 collective-permute-start.14
  118.9 3.8 collective-permute-start.13
  122.8 1.5 collective-permute-done.13
  124.5 7.6 %collective-permute-done.12 = bf16[4,128]{1,0:T(4,128)(2,1)S(1)} collective-permute-done((bf16[4,128]{1,0:T(4,128)(2,1)}, bf16[4,128]{1,0:T(4,128)(2,1)S(1)}, u32[]{:S(2)}, u32[]{:S(2)}) %collective-permute-start.12) | collective-permute-done | bytes 1056 | tf_op jit(solution)/shard_map/ppermute | solution.py:12
  132.1 1.7 collective-permute-start.11
  133.9 1.7 collective-permute-start.10
  135.6 3.8 collective-permute-start.9
  139.4 3.0 collective-permute-start.8
  143.5 1.8 scatter-add.54
  145.2 2.6 fusion.45
  147.9 2.2 broadcast_select_fusion.1
  150.1 2.4 scatter-add.56
  161.0 3.7 fusion.5
  164.7 2.0 convolution_bitcast_fusion.16
  166.6 2.0 convolution_bitcast_fusion.15
  168.6 1.9 convolution_bitcast_fusion.14
  170.5 2.0 convolution_bitcast_fusion.13
  172.5 2.0 convolution_bitcast_fusion.12
  174.5 1.9 convolution_bitcast_fusion.11
  176.4 2.0 convolution_bitcast_fusion.10
  178.4 2.0 convolution_bitcast_fusion.9
  180.4 2.3 convolution_bitcast_fusion.17
  183.7 3.1 convolution_select_fusion
  188.1 1.3 copy-done.4
  190.2 3.3 slice.1289
  194.8 3.9 fusion.71
  199.8 2.9 select_convert_fusion
  203.1 1.6 copy.147
  205.1 4.8 collective-permute-start.31
  209.9 4.1 collective-permute-start.28
  216.3 2.9 copy.152
  221.6 4.6 collective-permute-start.26
  243.2 1.4 collective-permute-start.24
  244.6 6.0 %collective-permute-start.27 = (f32[4,64,128]{2,1,0:T(8,128)S(1)}, f32[4,64,128]{2,1,0:T(8,128)S(1)}, u32[]{:S(2)}, u32[]{:S(2)}) collective-permute-start(f32[4,64,128]{2,1,0:T(8,128)S(1)} %copy-done.18), channel_id=1, source_target_pairs={{0,255},{1,0},{2,1},{3,2},{4,3},{5,4},{6,5},{7,6},{8,7},{9,8},{10,... | collective-permute-start | bytes 393224 | tf_op jit(solution)/shard_map/ppermute | solution.py:12
  250.7 2.5 collective-permute-done.27
  253.1 2.5 collective-permute-done.25
  260.5 1.6 copy.148
  262.2 243.9 %all-reduce.5.cloned.1.call-done = (f32[3,3,128,128]{3,2,1,0:T(8,128)}, f32[3,3,128,128]{3,2,1,0:T(8,128)}) async-done(((f32[3,3,128,128]{3,2,1,0:T(8,128)}, f32[3,3,128,128]{3,2,1,0:T(8,128)}), (f32[3,3,128,128]{3,2,1,0:T(8,128)}, f32[3,3,128,128]{3,2,1,0:T(8,128)})) %all-reduce.5.cloned.1.call-update) | async-done | bytes 1179664 | tf_op jit(solution)/shard_map/psum | solution.py:163
  506.0 1.9 broadcast_multiply_fusion.1
  508.0 1.9 broadcast_multiply_fusion
  (330 shorter events, 65.4 us)
Async XLA Ops:
  7.2 95.6 %copy-start = (bf16[3,3,128,128]{3,2,1,0:T(8,128)(2,1)S(1)}, bf16[3,3,128,128]{3,2,1,0:T(8,128)(2,1)}, u32[]{:S(2)}) copy-start(bf16[3,3,128,128]{3,2,1,0:T(8,128)(2,1)} %param.71) | copy-start | bytes 884740
  7.2 498.9 %all-reduce.5.cloned.1.call-start = ((), (), s32[]{:S(2)}) async-start(), calls=%async_computation | async-start | bytes 2359296 | tf_op jit(solution)/shard_map/psum | solution.py:163
  8.0 49.4 %collective-permute-start.7 = (bf16[4,128]{1,0:T(4,128)(2,1)S(1)}, bf16[4,128]{1,0:T(4,128)(2,1)S(1)}, u32[]{:S(2)}, u32[]{:S(2)}) collective-permute-start(bf16[4,128]{1,0:T(4,128)(2,1)S(1)} %pad_maximum_fusion.4), channel_id=1, source_target_pairs={{0,225},{1,226},{2,227},{3,228},{4,229},{5,230},{6,231},{7,232},{8... | collective-permute-start | bytes 3080 | tf_op jit(solution)/shard_map/ppermute | solution.py:12
  11.3 50.3 %collective-permute-start.6 = (bf16[4,128]{1,0:T(4,128)(2,1)S(1)}, bf16[4,128]{1,0:T(4,128)(2,1)S(1)}, u32[]{:S(2)}, u32[]{:S(2)}) collective-permute-start(bf16[4,128]{1,0:T(4,128)(2,1)S(1)} %pad_maximum_fusion.4), channel_id=1, source_target_pairs={{0,223},{1,224},{2,225},{3,226},{4,227},{5,228},{6,229},{7,230},{8... | collective-permute-start | bytes 3080 | tf_op jit(solution)/shard_map/ppermute | solution.py:12
  12.3 49.4 %collective-permute-start.5 = (bf16[4,128]{1,0:T(4,128)(2,1)S(1)}, bf16[4,128]{1,0:T(4,128)(2,1)S(1)}, u32[]{:S(2)}, u32[]{:S(2)}) collective-permute-start(bf16[4,128]{1,0:T(4,128)(2,1)S(1)} %pad_maximum_fusion.4), channel_id=1, source_target_pairs={{0,31},{1,32},{2,33},{3,34},{4,35},{5,36},{6,37},{7,38},{8,39},{9,... | collective-permute-start | bytes 3080 | tf_op jit(solution)/shard_map/ppermute | solution.py:12
  18.0 48.3 %collective-permute-start.4 = (bf16[4,128]{1,0:T(4,128)(2,1)S(1)}, bf16[4,128]{1,0:T(4,128)(2,1)S(1)}, u32[]{:S(2)}, u32[]{:S(2)}) collective-permute-start(bf16[4,128]{1,0:T(4,128)(2,1)S(1)} %pad_maximum_fusion.4), channel_id=1, source_target_pairs={{0,33},{1,34},{2,35},{3,36},{4,37},{5,38},{6,39},{7,40},{8,41},{9,... | collective-permute-start | bytes 3080 | tf_op jit(solution)/shard_map/ppermute | solution.py:12
  19.8 68.6 %collective-permute-start.3 = (bf16[4,64,128]{2,1,0:T(8,128)(2,1)S(1)}, bf16[4,64,128]{2,1,0:T(8,128)(2,1)}, u32[]{:S(2)}, u32[]{:S(2)}) collective-permute-start(bf16[4,64,128]{2,1,0:T(8,128)(2,1)S(1)} %pad_maximum_fusion.2), channel_id=1, source_target_pairs={{0,1},{1,2},{2,3},{3,4},{4,5},{5,6},{6,7},{7,8},{8,9},{9,10},{10,1... | collective-permute-start | bytes 196616 | tf_op jit(solution)/shard_map/ppermute | solution.py:12
  39.6 5.0 copy-start.40
  39.6 5.0 copy-start.41
  39.8 13.6 %copy-start.3 = (f32[1,66,66,128]{3,1,2,0:T(8,128)}, f32[1,66,66,128]{3,1,2,0:T(8,128)S(1)}, u32[]{:S(2)}) copy-start(f32[1,66,66,128]{3,1,2,0:T(8,128)S(1)} %slice_bitcast_fusion) | copy-start | bytes 6690820
  41.3 2.2 copy-start.32
  41.3 12.1 %copy-start.29 = (f32[4]{0:T(128)}, f32[4]{0:T(128)S(1)}, u32[]{:S(2)}) copy-start(f32[4]{0:T(128)S(1)} %compare_convert_fusion.7) | copy-start | bytes 52
  42.0 1.5 copy-start.34
  43.2 10.2 %copy-start.36 = (f32[4]{0:T(128)}, f32[4]{0:T(128)S(1)}, u32[]{:S(2)}) copy-start(f32[4]{0:T(128)S(1)} %compare_convert_fusion.3) | copy-start | bytes 52
  51.7 1.7 copy-start.16
  57.4 9.0 %collective-permute-start.20 = (f32[4,128]{1,0:T(4,128)S(1)}, f32[4,128]{1,0:T(4,128)S(1)}, u32[]{:S(2)}, u32[]{:S(2)}) collective-permute-start(f32[4,128]{1,0:T(4,128)S(1)} %broadcast_multiply_fusion.17), channel_id=1, source_target_pairs={{0,223},{1,224},{2,225},{3,226},{4,227},{5,228},{6,229},{7,230},{8... | collective-permute-start | bytes 6152 | tf_op jit(solution)/shard_map/ppermute | solution.py:12
  61.6 8.4 %collective-permute-start.22 = (f32[4,128]{1,0:T(4,128)S(1)}, f32[4,128]{1,0:T(4,128)S(1)}, u32[]{:S(2)}, u32[]{:S(2)}) collective-permute-start(f32[4,128]{1,0:T(4,128)S(1)} %broadcast_multiply_fusion.15), channel_id=1, source_target_pairs={{0,33},{1,34},{2,35},{3,36},{4,37},{5,38},{6,39},{7,40},{8,41},{9,... | collective-permute-start | bytes 6152 | tf_op jit(solution)/shard_map/ppermute | solution.py:12
  61.8 12.9 %collective-permute-start.23 = (f32[4,128]{1,0:T(4,128)S(1)}, f32[4,128]{1,0:T(4,128)S(1)}, u32[]{:S(2)}, u32[]{:S(2)}) collective-permute-start(f32[4,128]{1,0:T(4,128)S(1)} %broadcast_multiply_fusion.14), channel_id=1, source_target_pairs={{0,31},{1,32},{2,33},{3,34},{4,35},{5,36},{6,37},{7,38},{8,39},{9,... | collective-permute-start | bytes 6152 | tf_op jit(solution)/shard_map/ppermute | solution.py:12
  66.3 8.8 %collective-permute-start.21 = (f32[4,128]{1,0:T(4,128)S(1)}, f32[4,128]{1,0:T(4,128)S(1)}, u32[]{:S(2)}, u32[]{:S(2)}) collective-permute-start(f32[4,128]{1,0:T(4,128)S(1)} %broadcast_multiply_fusion.16), channel_id=1, source_target_pairs={{0,225},{1,226},{2,227},{3,228},{4,229},{5,230},{6,231},{7,232},{8... | collective-permute-start | bytes 6152 | tf_op jit(solution)/shard_map/ppermute | solution.py:12
  66.4 16.3 %collective-permute-start.2 = (bf16[4,64,128]{2,1,0:T(8,128)(2,1)S(1)}, bf16[4,64,128]{2,1,0:T(8,128)(2,1)S(1)}, u32[]{:S(2)}, u32[]{:S(2)}) collective-permute-start(bf16[4,64,128]{2,1,0:T(8,128)(2,1)S(1)} %pad_maximum_fusion.2), channel_id=1, source_target_pairs={{0,224},{1,225},{2,226},{3,227},{4,228},{5,229},{6,230},{7,231},{8... | collective-permute-start | bytes 196616 | tf_op jit(solution)/shard_map/ppermute | solution.py:12
  70.1 10.2 %collective-permute-start.1 = (bf16[4,64,128]{2,1,0:T(8,128)(2,1)S(1)}, bf16[4,64,128]{2,1,0:T(8,128)(2,1)S(1)}, u32[]{:S(2)}, u32[]{:S(2)}) collective-permute-start(bf16[4,64,128]{2,1,0:T(8,128)(2,1)S(1)} %pad_maximum_fusion.2), channel_id=1, source_target_pairs={{0,255},{1,0},{2,1},{3,2},{4,3},{5,4},{6,5},{7,6},{8,7},{9,8},{10,... | collective-permute-start | bytes 196616 | tf_op jit(solution)/shard_map/ppermute | solution.py:12
  74.6 8.0 %collective-permute-start = (bf16[4,64,128]{2,1,0:T(8,128)(2,1)S(1)}, bf16[4,64,128]{2,1,0:T(8,128)(2,1)S(1)}, u32[]{:S(2)}, u32[]{:S(2)}) collective-permute-start(bf16[4,64,128]{2,1,0:T(8,128)(2,1)S(1)} %pad_maximum_fusion.2), channel_id=1, source_target_pairs={{0,32},{1,33},{2,34},{3,35},{4,36},{5,37},{6,38},{7,39},{8,40},{9,... | collective-permute-start | bytes 196616 | tf_op jit(solution)/shard_map/ppermute | solution.py:12
  75.1 58.8 %collective-permute-start.19 = (f32[4,64,128]{2,1,0:T(8,128)}, f32[4,64,128]{2,1,0:T(8,128)S(1)}, u32[]{:S(2)}, u32[]{:S(2)}) collective-permute-start(f32[4,64,128]{2,1,0:T(8,128)} %broadcast_multiply_fusion.6), channel_id=1, source_target_pairs={{0,255},{1,0},{2,1},{3,2},{4,3},{5,4},{6,5},{7,6},{8,7},{9,8},{10,... | collective-permute-start | bytes 393224 | tf_op jit(solution)/shard_map/ppermute | solution.py:12
  80.2 55.4 %collective-permute-start.17 = (f32[4,64,128]{2,1,0:T(8,128)S(1)}, f32[4,64,128]{2,1,0:T(8,128)S(1)}, u32[]{:S(2)}, u32[]{:S(2)}) collective-permute-start(f32[4,64,128]{2,1,0:T(8,128)S(1)} %broadcast_multiply_fusion.8), channel_id=1, source_target_pairs={{0,1},{1,2},{2,3},{3,4},{4,5},{5,6},{6,7},{7,8},{8,9},{9,10},{10,1... | collective-permute-start | bytes 393224 | tf_op jit(solution)/shard_map/ppermute | solution.py:12
  82.6 56.8 %collective-permute-start.18 = (f32[4,64,128]{2,1,0:T(8,128)S(1)}, f32[4,64,128]{2,1,0:T(8,128)S(1)}, u32[]{:S(2)}, u32[]{:S(2)}) collective-permute-start(f32[4,64,128]{2,1,0:T(8,128)S(1)} %broadcast_multiply_fusion.7), channel_id=1, source_target_pairs={{0,32},{1,33},{2,34},{3,35},{4,36},{5,37},{6,38},{7,39},{8,40},{9,... | collective-permute-start | bytes 393224 | tf_op jit(solution)/shard_map/ppermute | solution.py:12
  82.7 59.7 %collective-permute-start.16 = (f32[4,64,128]{2,1,0:T(8,128)S(1)}, f32[4,64,128]{2,1,0:T(8,128)S(1)}, u32[]{:S(2)}, u32[]{:S(2)}) collective-permute-start(f32[4,64,128]{2,1,0:T(8,128)S(1)} %broadcast_multiply_fusion.9), channel_id=1, source_target_pairs={{0,224},{1,225},{2,226},{3,227},{4,228},{5,229},{6,230},{7,231},{8... | collective-permute-start | bytes 393224 | tf_op jit(solution)/shard_map/ppermute | solution.py:12
  109.2 6.0 %collective-permute-start.15 = (bf16[4,128]{1,0:T(4,128)(2,1)}, bf16[4,128]{1,0:T(4,128)(2,1)}, u32[]{:S(2)}, u32[]{:S(2)}) collective-permute-start(bf16[4,128]{1,0:T(4,128)(2,1)} %pad_maximum_fusion.5), channel_id=1, source_target_pairs={{0,225},{1,226},{2,227},{3,228},{4,229},{5,230},{6,231},{7,232},{8... | collective-permute-start | bytes 3080 | tf_op jit(solution)/shard_map/ppermute | solution.py:12
  109.3 1.7 copy-start.15
  111.0 2.3 copy-start.14
  113.3 40.6 %copy-start.31 = (f32[4,128]{1,0:T(4,128)S(1)}, f32[4,128]{1,0:T(4,128)}, u32[]{:S(2)}) copy-start(f32[4,128]{1,0:T(4,128)} %add_add_fusion.3) | copy-start | bytes 6148
  115.2 3.7 collective-permute-start.14
  118.9 5.4 %collective-permute-start.13 = (bf16[4,128]{1,0:T(4,128)(2,1)}, bf16[4,128]{1,0:T(4,128)(2,1)S(1)}, u32[]{:S(2)}, u32[]{:S(2)}) collective-permute-start(bf16[4,128]{1,0:T(4,128)(2,1)} %pad_maximum_fusion.5), channel_id=1, source_target_pairs={{0,31},{1,32},{2,33},{3,34},{4,35},{5,36},{6,37},{7,38},{8,39},{9,... | collective-permute-start | bytes 3080 | tf_op jit(solution)/shard_map/ppermute | solution.py:12
  124.3 7.9 %collective-permute-start.12 = (bf16[4,128]{1,0:T(4,128)(2,1)}, bf16[4,128]{1,0:T(4,128)(2,1)S(1)}, u32[]{:S(2)}, u32[]{:S(2)}) collective-permute-start(bf16[4,128]{1,0:T(4,128)(2,1)} %pad_maximum_fusion.5), channel_id=1, source_target_pairs={{0,33},{1,34},{2,35},{3,36},{4,37},{5,38},{6,39},{7,40},{8,41},{9,... | collective-permute-start | bytes 3080 | tf_op jit(solution)/shard_map/ppermute | solution.py:12
  132.1 61.4 %collective-permute-start.11 = (bf16[4,64,128]{2,1,0:T(8,128)(2,1)S(1)}, bf16[4,64,128]{2,1,0:T(8,128)(2,1)S(1)}, u32[]{:S(2)}, u32[]{:S(2)}) collective-permute-start(bf16[4,64,128]{2,1,0:T(8,128)(2,1)S(1)} %pad_maximum_fusion.3), channel_id=1, source_target_pairs={{0,1},{1,2},{2,3},{3,4},{4,5},{5,6},{6,7},{7,8},{8,9},{9,10},{10,1... | collective-permute-start | bytes 196616 | tf_op jit(solution)/shard_map/ppermute | solution.py:12
  133.9 55.6 %collective-permute-start.10 = (bf16[4,64,128]{2,1,0:T(8,128)(2,1)S(1)}, bf16[4,64,128]{2,1,0:T(8,128)(2,1)S(1)}, u32[]{:S(2)}, u32[]{:S(2)}) collective-permute-start(bf16[4,64,128]{2,1,0:T(8,128)(2,1)S(1)} %pad_maximum_fusion.3), channel_id=1, source_target_pairs={{0,224},{1,225},{2,226},{3,227},{4,228},{5,229},{6,230},{7,231},{8... | collective-permute-start | bytes 196616 | tf_op jit(solution)/shard_map/ppermute | solution.py:12
  135.6 58.0 %collective-permute-start.9 = (bf16[4,64,128]{2,1,0:T(8,128)(2,1)S(1)}, bf16[4,64,128]{2,1,0:T(8,128)(2,1)S(1)}, u32[]{:S(2)}, u32[]{:S(2)}) collective-permute-start(bf16[4,64,128]{2,1,0:T(8,128)(2,1)S(1)} %pad_maximum_fusion.3), channel_id=1, source_target_pairs={{0,255},{1,0},{2,1},{3,2},{4,3},{5,4},{6,5},{7,6},{8,7},{9,8},{10,... | collective-permute-start | bytes 196616 | tf_op jit(solution)/shard_map/ppermute | solution.py:12
  139.4 54.2 %collective-permute-start.8 = (bf16[4,64,128]{2,1,0:T(8,128)(2,1)S(1)}, bf16[4,64,128]{2,1,0:T(8,128)(2,1)S(1)}, u32[]{:S(2)}, u32[]{:S(2)}) collective-permute-start(bf16[4,64,128]{2,1,0:T(8,128)(2,1)S(1)} %pad_maximum_fusion.3), channel_id=1, source_target_pairs={{0,32},{1,33},{2,34},{3,35},{4,36},{5,37},{6,38},{7,39},{8,40},{9,... | collective-permute-start | bytes 196616 | tf_op jit(solution)/shard_map/ppermute | solution.py:12
  161.0 3.7 copy-start.5
  188.0 1.4 copy-start.4
  203.0 1.8 copy-start.39
  203.0 1.8 copy-start.37
  203.0 1.9 copy-start.35
  203.0 2.0 copy-start.33
  205.1 38.1 %collective-permute-start.31 = (f32[4,128]{1,0:T(4,128)S(1)}, f32[4,128]{1,0:T(4,128)S(1)}, u32[]{:S(2)}, u32[]{:S(2)}) collective-permute-start(f32[4,128]{1,0:T(4,128)S(1)} %broadcast_multiply_fusion.10), channel_id=1, source_target_pairs={{0,31},{1,32},{2,33},{3,34},{4,35},{5,36},{6,37},{7,38},{8,39},{9,... | collective-permute-start | bytes 6152 | tf_op jit(solution)/shard_map/ppermute | solution.py:12
  209.9 34.6 %collective-permute-start.30 = (f32[4,128]{1,0:T(4,128)S(1)}, f32[4,128]{1,0:T(4,128)S(1)}, u32[]{:S(2)}, u32[]{:S(2)}) collective-permute-start(f32[4,128]{1,0:T(4,128)S(1)} %broadcast_multiply_fusion.11), channel_id=1, source_target_pairs={{0,33},{1,34},{2,35},{3,36},{4,37},{5,38},{6,39},{7,40},{8,41},{9,... | collective-permute-start | bytes 6152 | tf_op jit(solution)/shard_map/ppermute | solution.py:12
  209.9 40.7 %collective-permute-start.28 = (f32[4,128]{1,0:T(4,128)S(1)}, f32[4,128]{1,0:T(4,128)S(1)}, u32[]{:S(2)}, u32[]{:S(2)}) collective-permute-start(f32[4,128]{1,0:T(4,128)S(1)} %broadcast_multiply_fusion.13), channel_id=1, source_target_pairs={{0,223},{1,224},{2,225},{3,226},{4,227},{5,228},{6,229},{7,230},{8... | collective-permute-start | bytes 6152 | tf_op jit(solution)/shard_map/ppermute | solution.py:12
  214.1 36.6 %collective-permute-start.29 = (f32[4,128]{1,0:T(4,128)S(1)}, f32[4,128]{1,0:T(4,128)S(1)}, u32[]{:S(2)}, u32[]{:S(2)}) collective-permute-start(f32[4,128]{1,0:T(4,128)S(1)} %broadcast_multiply_fusion.12), channel_id=1, source_target_pairs={{0,225},{1,226},{2,227},{3,228},{4,229},{5,230},{6,231},{7,232},{8... | collective-permute-start | bytes 6152 | tf_op jit(solution)/shard_map/ppermute | solution.py:12
  216.3 3.8 copy-start.30
  216.3 9.8 %copy-start.13 = (bf16[1,64,64,128]{3,1,2,0:T(8,128)(2,1)S(1)}, bf16[1,64,64,128]{3,1,2,0:T(8,128)(2,1)}, u32[]{:S(2)}) copy-start(bf16[1,64,64,128]{3,1,2,0:T(8,128)(2,1)} %get-tuple-element.426) | copy-start | bytes 3145732
  219.2 7.6 %copy-start.12 = (bf16[1,64,64,128]{3,1,2,0:T(8,128)(2,1)S(1)}, bf16[1,64,64,128]{3,1,2,0:T(8,128)(2,1)}, u32[]{:S(2)}) copy-start(bf16[1,64,64,128]{3,1,2,0:T(8,128)(2,1)} %get-tuple-element.427) | copy-start | bytes 3145732
  221.6 29.1 %collective-permute-start.26 = (f32[4,64,128]{2,1,0:T(8,128)}, f32[4,64,128]{2,1,0:T(8,128)}, u32[]{:S(2)}, u32[]{:S(2)}) collective-permute-start(f32[4,64,128]{2,1,0:T(8,128)} %broadcast_multiply_fusion.3), channel_id=1, source_target_pairs={{0,32},{1,33},{2,34},{3,35},{4,36},{5,37},{6,38},{7,39},{8,40},{9,... | collective-permute-start | bytes 393224 | tf_op jit(solution)/shard_map/ppermute | solution.py:12
  226.1 1.4 copy-start.2
  239.9 1.3 copy-start.20
  240.0 1.3 copy-start.21
  240.0 1.3 copy-start.22
  240.0 1.3 copy-start.23
  240.0 1.3 copy-start.24
  241.3 1.9 copy-start.19
  241.4 3.2 copy-start.18
  241.4 9.3 %copy-start.17 = (f32[4,64,128]{2,1,0:T(8,128)S(1)}, f32[4,64,128]{2,1,0:T(8,128)}, u32[]{:S(2)}) copy-start(f32[4,64,128]{2,1,0:T(8,128)} %broadcast_multiply_fusion.4) | copy-start | bytes 393220
  243.2 7.5 %collective-permute-start.24 = (f32[4,64,128]{2,1,0:T(8,128)S(1)}, f32[4,64,128]{2,1,0:T(8,128)S(1)}, u32[]{:S(2)}, u32[]{:S(2)}) collective-permute-start(f32[4,64,128]{2,1,0:T(8,128)S(1)} %copy-done.19), channel_id=1, source_target_pairs={{0,224},{1,225},{2,226},{3,227},{4,228},{5,229},{6,230},{7,231},{8... | collective-permute-start | bytes 393224 | tf_op jit(solution)/shard_map/ppermute | solution.py:12
  244.6 8.6 %collective-permute-start.27 = (f32[4,64,128]{2,1,0:T(8,128)S(1)}, f32[4,64,128]{2,1,0:T(8,128)S(1)}, u32[]{:S(2)}, u32[]{:S(2)}) collective-permute-start(f32[4,64,128]{2,1,0:T(8,128)S(1)} %copy-done.18), channel_id=1, source_target_pairs={{0,255},{1,0},{2,1},{3,2},{4,3},{5,4},{6,5},{7,6},{8,7},{9,8},{10,... | collective-permute-start | bytes 393224 | tf_op jit(solution)/shard_map/ppermute | solution.py:12
  250.6 5.0 collective-permute-start.25
  260.3 249.6 %copy-start.1 = (bf16[3,3,128,128]{3,2,1,0:T(8,128)(2,1)S(1)}, bf16[3,3,128,128]{3,2,1,0:T(8,128)(2,1)}, u32[]{:S(2)}) copy-start(bf16[3,3,128,128]{3,2,1,0:T(8,128)(2,1)} %param.71) | copy-start | bytes 884740
  (17 other events, 18.9 us)
Sparse Core Ops, SparseCore 0:
  243.3 262.6 all-reduce.4
where the time goes:
time: 523 us; the launch traced here: 517 us
  waiting for transfers between devices  261 us (50%)
  starting transfers between devices  76.6 us (15%)
  local copies, waits for them, and re-layouts  75.6 us (14%)
  matrix products  36.5 us (7%)
  other arithmetic  33.6 us (6%)
  between operations  33.5 us (6%)
    psum x1, waiting for transfers between devices, local(): grad_one, grad_two = lax.psum((grad_one, grad_two), ('face', 'sub'))  244 us
    ppermute x32, starting transfers between devices, shifted(): return lax.ppermute(x, axis, [(i, (i + by) % size) for i in range(size)])  76.6 us
    dot_general x18, matrix products, conv_kernel(): lax.dot_general(window, flat_up, (((0,), (0,)), ((), ())), preferred_elem...  22.3 us
    unnamed x104, local copies, waits for them, and re-layouts  20.4 us
    ppermute x32, waiting for transfers between devices, shifted(): return lax.ppermute(x, axis, [(i, (i + by) % size) for i in range(size)])  17.3 us
  transfers between devices with their start and end apart: 33, of which 7 were waited for; matrix products, arithmetic and copies ran while one was open for 24% of the time, Pallas kernels for 0%

commit v1 on v0

--- a/solution.py
+++ b/solution.py
@@ -160,7 +160,7 @@
     grad_fields = return_halo(conv_inputs(grad_pre, kernel_one), edge_codes, corner_codes).astype(
         jnp.bfloat16
     )
-    grad_one, grad_two = lax.psum((grad_one, grad_two), ("face", "sub"))
+    grad_one, grad_two = lax.psum(lax.psum((grad_one, grad_two), "sub"), "face")
     return (outputs[None], grad_fields[None], grad_one * norm_factor, grad_two * norm_factor)
 
 

time: 523 us -> 1520 us (2.91)
  waiting for transfers between devices: 261 us -> 1260 us
    psum x1 -> x2, waiting for transfers between devices: 244 us -> 1240 us  [local(): grad_one, grad_two = lax.psum(lax.psum((grad_one, grad_two), 'sub'), 'face')]
  transfers between devices with their start and end apart: 33 -> 34, of which waited for: 7 -> 8; matrix products, arithmetic and copies ran while one was open for 24% -> 8% of each run, Pallas kernels for 0% -> 0%
where the time goes in v1:
time: 1520 us; the launch traced here: 1510 us
  waiting for transfers between devices  1260 us (83%)
  starting transfers between devices  76.7 us (5%)
  local copies, waits for them, and re-layouts  75.7 us (5%)
  matrix products  36.6 us (2%)
  between operations  34 us (2%)
  other arithmetic  33.8 us (2%)
    psum x2, waiting for transfers between devices, local(): grad_one, grad_two = lax.psum(lax.psum((grad_one, grad_two), 'sub'), 'face')  1240 us
    ppermute x32, starting transfers between devices, shifted(): return lax.ppermute(x, axis, [(i, (i + by) % size) for i in range(size)])  76.6 us
  transfers between devices with their start and end apart: 34, of which 8 were waited for; matrix products, arithmetic and copies ran while one was open for 8% of the time, Pallas kernels for 0%

profile of v1, /device:TPU:8, one launch (start us, length us, event | category | flops | bytes accessed | tf_op | source)
XLA Modules:
  0.0 1511.7 jit_solution(16696833411178759197)
XLA Ops:
  8.0 3.3 collective-permute-start.7
  12.3 5.7 collective-permute-start.5
  33.2 1.9 copy.179
  36.2 3.1 convolution_select_fusion.1
  45.0 2.0 and_reduce_fusion
  52.1 1.7 slice.1266
  53.8 1.5 pad.122
  57.9 4.2 collective-permute-start.20
  62.2 4.5 collective-permute-start.23
  66.9 3.7 collective-permute-start.2
  70.5 4.6 collective-permute-start.1
  75.5 4.6 collective-permute-start.19
  80.8 2.3 collective-permute-done
  83.2 5.7 collective-permute-start.16
  90.4 1.4 scatter.54
  91.8 1.7 scatter.55
  93.5 1.4 scatter.56
  94.9 1.7 scatter.59
  101.6 1.4 copy.155
  103.8 5.0 add_divide_fusion
  111.6 1.8 copy.116
  113.9 1.9 copy.117
  115.8 2.2 collective-permute-start.14
  119.5 3.8 collective-permute-start.13
  123.4 1.5 collective-permute-done.13
  125.1 7.6 collective-permute-done.12
  132.7 1.9 collective-permute-start.11
  134.6 1.7 collective-permute-start.10
  136.3 3.6 collective-permute-start.9
  140.0 3.0 collective-permute-start.8
  144.1 1.8 scatter-add.54
  145.8 2.6 fusion.45
  148.5 2.3 broadcast_select_fusion.1
  150.8 2.4 scatter-add.56
  161.7 3.7 fusion.5
  165.3 2.0 convolution_bitcast_fusion.16
  167.3 2.0 convolution_bitcast_fusion.15
  169.3 1.9 convolution_bitcast_fusion.14
  171.2 2.0 convolution_bitcast_fusion.13
  173.2 2.0 convolution_bitcast_fusion.12
  175.2 1.9 convolution_bitcast_fusion.11
  177.1 2.0 convolution_bitcast_fusion.10
  179.1 2.0 convolution_bitcast_fusion.9
  181.1 2.3 convolution_bitcast_fusion.17
  184.4 3.1 convolution_select_fusion
  188.8 1.3 copy-done.4
  190.9 3.3 slice.1289
  195.5 3.9 fusion.71
  200.5 2.9 select_convert_fusion
  203.9 1.6 copy.147
  205.8 4.8 collective-permute-start.31
  210.6 4.1 collective-permute-start.28
  217.0 2.9 copy.152
  222.3 4.5 collective-permute-start.26
  244.0 1.4 collective-permute-start.24
  245.3 6.0 collective-permute-start.27
  251.4 2.5 collective-permute-done.27
  253.9 2.5 collective-permute-done.25
  258.8 1.4 broadcast_select_fusion
  261.0 40.5 %all-reduce.9.cloned.1.call-done = (f32[3,3,128,128]{3,2,1,0:T(8,128)}, f32[3,3,128,128]{3,2,1,0:T(8,128)}) async-done(((f32[3,3,128,128]{3,2,1,0:T(8,128)}, f32[3,3,128,128]{3,2,1,0:T(8,128)}), (f32[3,3,128,128]{3,2,1,0:T(8,128)}, f32[3,3,128,128]{3,2,1,0:T(8,128)})) %all-reduce.9.cloned.1.call-update) | async-done | bytes 1179664 | tf_op jit(solution)/shard_map/psum | solution.py:163
  301.9 1.6 copy.148
  303.6 1197.2 %all-reduce.7.cloned.1.call-done = (f32[3,3,128,128]{3,2,1,0:T(8,128)}, f32[3,3,128,128]{3,2,1,0:T(8,128)}) async-done(((f32[3,3,128,128]{3,2,1,0:T(8,128)}, f32[3,3,128,128]{3,2,1,0:T(8,128)}), (f32[3,3,128,128]{3,2,1,0:T(8,128)}, f32[3,3,128,128]{3,2,1,0:T(8,128)})) %all-reduce.7.cloned.1.call-update) | async-done | bytes 1179664 | tf_op jit(solution)/shard_map/psum | solution.py:163
  1500.7 1.9 broadcast_multiply_fusion.1
  1502.7 1.9 broadcast_multiply_fusion
  (333 shorter events, 66.9 us)
Async XLA Ops:
  7.2 96.2 %copy-start = (bf16[3,3,128,128]{3,2,1,0:T(8,128)(2,1)S(1)}, bf16[3,3,128,128]{3,2,1,0:T(8,128)(2,1)}, u32[]{:S(2)}) copy-start(bf16[3,3,128,128]{3,2,1,0:T(8,128)(2,1)} %param.71) | copy-start | bytes 884740
  7.2 294.3 %all-reduce.9.cloned.1.call-start = ((), (), s32[]{:S(2)}) async-start(), calls=%async_computation.1 | async-start | bytes 2359296 | tf_op jit(solution)/shard_map/psum | solution.py:163
  8.0 49.9 %collective-permute-start.7 = (bf16[4,128]{1,0:T(4,128)(2,1)S(1)}, bf16[4,128]{1,0:T(4,128)(2,1)S(1)}, u32[]{:S(2)}, u32[]{:S(2)}) collective-permute-start(bf16[4,128]{1,0:T(4,128)(2,1)S(1)} %pad_maximum_fusion.4), channel_id=1, source_target_pairs={{0,225},{1,226},{2,227},{3,228},{4,229},{5,230},{6,231},{7,232},{8... | collective-permute-start | bytes 3080 | tf_op jit(solution)/shard_map/ppermute | solution.py:12
  11.3 50.8 %collective-permute-start.6 = (bf16[4,128]{1,0:T(4,128)(2,1)S(1)}, bf16[4,128]{1,0:T(4,128)(2,1)S(1)}, u32[]{:S(2)}, u32[]{:S(2)}) collective-permute-start(bf16[4,128]{1,0:T(4,128)(2,1)S(1)} %pad_maximum_fusion.4), channel_id=1, source_target_pairs={{0,223},{1,224},{2,225},{3,226},{4,227},{5,228},{6,229},{7,230},{8... | collective-permute-start | bytes 3080 | tf_op jit(solution)/shard_map/ppermute | solution.py:12
  12.3 49.9 %collective-permute-start.5 = (bf16[4,128]{1,0:T(4,128)(2,1)S(1)}, bf16[4,128]{1,0:T(4,128)(2,1)S(1)}, u32[]{:S(2)}, u32[]{:S(2)}) collective-permute-start(bf16[4,128]{1,0:T(4,128)(2,1)S(1)} %pad_maximum_fusion.4), channel_id=1, source_target_pairs={{0,31},{1,32},{2,33},{3,34},{4,35},{5,36},{6,37},{7,38},{8,39},{9,... | collective-permute-start | bytes 3080 | tf_op jit(solution)/shard_map/ppermute | solution.py:12
  18.0 48.7 %collective-permute-start.4 = (bf16[4,128]{1,0:T(4,128)(2,1)S(1)}, bf16[4,128]{1,0:T(4,128)(2,1)S(1)}, u32[]{:S(2)}, u32[]{:S(2)}) collective-permute-start(bf16[4,128]{1,0:T(4,128)(2,1)S(1)} %pad_maximum_fusion.4), channel_id=1, source_target_pairs={{0,33},{1,34},{2,35},{3,36},{4,37},{5,38},{6,39},{7,40},{8,41},{9,... | collective-permute-start | bytes 3080 | tf_op jit(solution)/shard_map/ppermute | solution.py:12
  19.8 69.1 %collective-permute-start.3 = (bf16[4,64,128]{2,1,0:T(8,128)(2,1)S(1)}, bf16[4,64,128]{2,1,0:T(8,128)(2,1)}, u32[]{:S(2)}, u32[]{:S(2)}) collective-permute-start(bf16[4,64,128]{2,1,0:T(8,128)(2,1)S(1)} %pad_maximum_fusion.2), channel_id=1, source_target_pairs={{0,1},{1,2},{2,3},{3,4},{4,5},{5,6},{6,7},{7,8},{8,9},{9,10},{10,1... | collective-permute-start | bytes 196616 | tf_op jit(solution)/shard_map/ppermute | solution.py:12
  39.9 5.1 copy-start.40
  39.9 5.1 copy-start.41
  40.1 13.8 copy-start.3
  41.6 2.2 copy-start.32
  41.6 12.2 copy-start.29
  42.3 1.6 copy-start.34
  43.6 10.2 copy-start.36
  52.1 1.7 copy-start.16
  57.9 9.0 collective-permute-start.20
  62.1 8.4 collective-permute-start.22
  62.2 12.9 collective-permute-start.23
  66.7 8.8 collective-permute-start.21
  66.9 16.3 %collective-permute-start.2 = (bf16[4,64,128]{2,1,0:T(8,128)(2,1)S(1)}, bf16[4,64,128]{2,1,0:T(8,128)(2,1)S(1)}, u32[]{:S(2)}, u32[]{:S(2)}) collective-permute-start(bf16[4,64,128]{2,1,0:T(8,128)(2,1)S(1)} %pad_maximum_fusion.2), channel_id=1, source_target_pairs={{0,224},{1,225},{2,226},{3,227},{4,228},{5,229},{6,230},{7,231},{8... | collective-permute-start | bytes 196616 | tf_op jit(solution)/shard_map/ppermute | solution.py:12
  70.5 10.2 collective-permute-start.1
  75.1 8.0 collective-permute-start
  75.5 59.1 %collective-permute-start.19 = (f32[4,64,128]{2,1,0:T(8,128)}, f32[4,64,128]{2,1,0:T(8,128)S(1)}, u32[]{:S(2)}, u32[]{:S(2)}) collective-permute-start(f32[4,64,128]{2,1,0:T(8,128)} %broadcast_multiply_fusion.6), channel_id=1, source_target_pairs={{0,255},{1,0},{2,1},{3,2},{4,3},{5,4},{6,5},{7,6},{8,7},{9,8},{10,... | collective-permute-start | bytes 393224 | tf_op jit(solution)/shard_map/ppermute | solution.py:12
  80.7 55.6 %collective-permute-start.17 = (f32[4,64,128]{2,1,0:T(8,128)S(1)}, f32[4,64,128]{2,1,0:T(8,128)S(1)}, u32[]{:S(2)}, u32[]{:S(2)}) collective-permute-start(f32[4,64,128]{2,1,0:T(8,128)S(1)} %broadcast_multiply_fusion.8), channel_id=1, source_target_pairs={{0,1},{1,2},{2,3},{3,4},{4,5},{5,6},{6,7},{7,8},{8,9},{9,10},{10,1... | collective-permute-start | bytes 393224 | tf_op jit(solution)/shard_map/ppermute | solution.py:12
  83.1 56.9 %collective-permute-start.18 = (f32[4,64,128]{2,1,0:T(8,128)S(1)}, f32[4,64,128]{2,1,0:T(8,128)S(1)}, u32[]{:S(2)}, u32[]{:S(2)}) collective-permute-start(f32[4,64,128]{2,1,0:T(8,128)S(1)} %broadcast_multiply_fusion.7), channel_id=1, source_target_pairs={{0,32},{1,33},{2,34},{3,35},{4,36},{5,37},{6,38},{7,39},{8,40},{9,... | collective-permute-start | bytes 393224 | tf_op jit(solution)/shard_map/ppermute | solution.py:12
  83.2 59.9 %collective-permute-start.16 = (f32[4,64,128]{2,1,0:T(8,128)S(1)}, f32[4,64,128]{2,1,0:T(8,128)S(1)}, u32[]{:S(2)}, u32[]{:S(2)}) collective-permute-start(f32[4,64,128]{2,1,0:T(8,128)S(1)} %broadcast_multiply_fusion.9), channel_id=1, source_target_pairs={{0,224},{1,225},{2,226},{3,227},{4,228},{5,229},{6,230},{7,231},{8... | collective-permute-start | bytes 393224 | tf_op jit(solution)/shard_map/ppermute | solution.py:12
  109.8 6.0 collective-permute-start.15
  109.9 1.7 copy-start.15
  111.5 2.3 copy-start.14
  113.9 40.7 %copy-start.31 = (f32[4,128]{1,0:T(4,128)S(1)}, f32[4,128]{1,0:T(4,128)}, u32[]{:S(2)}) copy-start(f32[4,128]{1,0:T(4,128)} %add_add_fusion.3) | copy-start | bytes 6148
  115.8 3.7 collective-permute-start.14
  119.5 5.4 collective-permute-start.13
  124.9 7.9 collective-permute-start.12
  132.7 61.5 %collective-permute-start.11 = (bf16[4,64,128]{2,1,0:T(8,128)(2,1)S(1)}, bf16[4,64,128]{2,1,0:T(8,128)(2,1)S(1)}, u32[]{:S(2)}, u32[]{:S(2)}) collective-permute-start(bf16[4,64,128]{2,1,0:T(8,128)(2,1)S(1)} %pad_maximum_fusion.3), channel_id=1, source_target_pairs={{0,1},{1,2},{2,3},{3,4},{4,5},{5,6},{6,7},{7,8},{8,9},{9,10},{10,1... | collective-permute-start | bytes 196616 | tf_op jit(solution)/shard_map/ppermute | solution.py:12
  134.6 55.5 %collective-permute-start.10 = (bf16[4,64,128]{2,1,0:T(8,128)(2,1)S(1)}, bf16[4,64,128]{2,1,0:T(8,128)(2,1)S(1)}, u32[]{:S(2)}, u32[]{:S(2)}) collective-permute-start(bf16[4,64,128]{2,1,0:T(8,128)(2,1)S(1)} %pad_maximum_fusion.3), channel_id=1, source_target_pairs={{0,224},{1,225},{2,226},{3,227},{4,228},{5,229},{6,230},{7,231},{8... | collective-permute-start | bytes 196616 | tf_op jit(solution)/shard_map/ppermute | solution.py:12
  136.3 58.0 %collective-permute-start.9 = (bf16[4,64,128]{2,1,0:T(8,128)(2,1)S(1)}, bf16[4,64,128]{2,1,0:T(8,128)(2,1)S(1)}, u32[]{:S(2)}, u32[]{:S(2)}) collective-permute-start(bf16[4,64,128]{2,1,0:T(8,128)(2,1)S(1)} %pad_maximum_fusion.3), channel_id=1, source_target_pairs={{0,255},{1,0},{2,1},{3,2},{4,3},{5,4},{6,5},{7,6},{8,7},{9,8},{10,... | collective-permute-start | bytes 196616 | tf_op jit(solution)/shard_map/ppermute | solution.py:12
  140.0 54.4 %collective-permute-start.8 = (bf16[4,64,128]{2,1,0:T(8,128)(2,1)S(1)}, bf16[4,64,128]{2,1,0:T(8,128)(2,1)S(1)}, u32[]{:S(2)}, u32[]{:S(2)}) collective-permute-start(bf16[4,64,128]{2,1,0:T(8,128)(2,1)S(1)} %pad_maximum_fusion.3), channel_id=1, source_target_pairs={{0,32},{1,33},{2,34},{3,35},{4,36},{5,37},{6,38},{7,39},{8,40},{9,... | collective-permute-start | bytes 196616 | tf_op jit(solution)/shard_map/ppermute | solution.py:12
  161.7 3.7 copy-start.5
  188.7 1.4 copy-start.4
  203.7 1.8 copy-start.39
  203.7 1.8 copy-start.37
  203.8 1.9 copy-start.35
  203.8 2.0 copy-start.33
  205.8 38.1 %collective-permute-start.31 = (f32[4,128]{1,0:T(4,128)S(1)}, f32[4,128]{1,0:T(4,128)S(1)}, u32[]{:S(2)}, u32[]{:S(2)}) collective-permute-start(f32[4,128]{1,0:T(4,128)S(1)} %broadcast_multiply_fusion.10), channel_id=1, source_target_pairs={{0,31},{1,32},{2,33},{3,34},{4,35},{5,36},{6,37},{7,38},{8,39},{9,... | collective-permute-start | bytes 6152 | tf_op jit(solution)/shard_map/ppermute | solution.py:12
  210.6 34.7 %collective-permute-start.30 = (f32[4,128]{1,0:T(4,128)S(1)}, f32[4,128]{1,0:T(4,128)S(1)}, u32[]{:S(2)}, u32[]{:S(2)}) collective-permute-start(f32[4,128]{1,0:T(4,128)S(1)} %broadcast_multiply_fusion.11), channel_id=1, source_target_pairs={{0,33},{1,34},{2,35},{3,36},{4,37},{5,38},{6,39},{7,40},{8,41},{9,... | collective-permute-start | bytes 6152 | tf_op jit(solution)/shard_map/ppermute | solution.py:12
  210.6 40.7 %collective-permute-start.28 = (f32[4,128]{1,0:T(4,128)S(1)}, f32[4,128]{1,0:T(4,128)S(1)}, u32[]{:S(2)}, u32[]{:S(2)}) collective-permute-start(f32[4,128]{1,0:T(4,128)S(1)} %broadcast_multiply_fusion.13), channel_id=1, source_target_pairs={{0,223},{1,224},{2,225},{3,226},{4,227},{5,228},{6,229},{7,230},{8... | collective-permute-start | bytes 6152 | tf_op jit(solution)/shard_map/ppermute | solution.py:12
  214.8 36.6 %collective-permute-start.29 = (f32[4,128]{1,0:T(4,128)S(1)}, f32[4,128]{1,0:T(4,128)S(1)}, u32[]{:S(2)}, u32[]{:S(2)}) collective-permute-start(f32[4,128]{1,0:T(4,128)S(1)} %broadcast_multiply_fusion.12), channel_id=1, source_target_pairs={{0,225},{1,226},{2,227},{3,228},{4,229},{5,230},{6,231},{7,232},{8... | collective-permute-start | bytes 6152 | tf_op jit(solution)/shard_map/ppermute | solution.py:12
  217.0 3.8 copy-start.30
  217.0 9.8 copy-start.13
  219.9 7.6 copy-start.12
  222.3 29.1 %collective-permute-start.26 = (f32[4,64,128]{2,1,0:T(8,128)}, f32[4,64,128]{2,1,0:T(8,128)}, u32[]{:S(2)}, u32[]{:S(2)}) collective-permute-start(f32[4,64,128]{2,1,0:T(8,128)} %broadcast_multiply_fusion.3), channel_id=1, source_target_pairs={{0,32},{1,33},{2,34},{3,35},{4,36},{5,37},{6,38},{7,39},{8,40},{9,... | collective-permute-start | bytes 393224 | tf_op jit(solution)/shard_map/ppermute | solution.py:12
  226.8 1.4 copy-start.2
  240.6 1.3 copy-start.20
  240.7 1.3 copy-start.22
  240.7 1.3 copy-start.23
  240.7 1.3 copy-start.24
  242.0 1.9 copy-start.19
  242.1 3.3 copy-start.18
  242.1 9.3 copy-start.17
  243.9 1256.9 %all-reduce.7.cloned.1.call-start = ((), (), s32[]{:S(2)}) async-start(), calls=%async_computation | async-start | bytes 2359296 | tf_op jit(solution)/shard_map/psum | solution.py:163
  244.0 7.5 collective-permute-start.24
  245.3 8.6 collective-permute-start.27
  251.4 5.0 collective-permute-start.25
  301.7 1202.9 %copy-start.1 = (bf16[3,3,128,128]{3,2,1,0:T(8,128)(2,1)S(1)}, bf16[3,3,128,128]{3,2,1,0:T(8,128)(2,1)}, u32[]{:S(2)}) copy-start(bf16[3,3,128,128]{3,2,1,0:T(8,128)(2,1)} %param.71) | copy-start | bytes 884740
  (18 other events, 20.2 us)
Sparse Core Ops, SparseCore 0:
  244.0 57.4 all-reduce.8
  304.4 1196.2 all-reduce.6
